TPU v7x, 32 devices: a whole 2x2x4 slice. The times are simulated.
32 devices in a mesh: groups: 2 (over x), ctx: 8 (over z, y), width: 2 (over core).
Axes of the slice: x: 2, y: 2, z: 4, core: 2. Of those that a mesh axis runs over, the one named last changes fastest.
Arguments:
- gating_vectors: bfloat16 [2048, 4096], P(('groups', 'ctx'), 'width'), parts along dimension 0, may hold values from -3 to 3
- lookup_vectors: bfloat16 [2048, 4096], P(('groups', 'ctx'), 'width'), parts along dimension 0, may hold values from -3 to 3
- payload_vectors: bfloat16 [2048, 4096], P(('groups', 'ctx'), 'width'), parts along dimension 0, may hold values from -6 to 6
- forgetting_exponent: bfloat16 [2048, 4096], P(('groups', 'ctx'), 'width'), parts along dimension 0, may hold values from 0 to 0.5
- inline_adapt_factor: bfloat16 [2048, 4096], P(('groups', 'ctx'), 'width'), parts along dimension 0, may hold values from 0 to 0.9
- group_layer_scaling: float32 [4096], P('width'), may hold values from 0.5 to 1.5
- group_layer_offset: float32 [4096], P('width'), may hold values from -3 to 3
- present_reward_factor: float32 [4096], P('width'), may hold values from -1 to 1
- shared_dictionary_matrix: bfloat16 [16384, 4096], P('ctx', 'width'), may hold values from -0.09375 to 0.09375
- sparse_code_offset: float32 [16384], P('ctx'), may hold values from -3 to 3
- reconstruct_offset: float32 [4096], P('width'), may hold values from -2 to 2
- panel_holder_choice: int32 [256, 2], P(('groups', 'ctx')), parts along dimension 0, may hold values from 0 to 7, all different within a row; in each aligned block of 16 rows (0 to 15, 16 to 31, ...) at most 8 rows name the same one
- holder_group_enabled: int32 [256, 2, 16], P(('groups', 'ctx')), parts along dimension 0, may hold values 0 or 1
- fixed_feature_slot: int32 [128], P('ctx'), may hold values from 0 to 127
- fixed_feature_amount: float32 [128], P('ctx'), may hold values from 2 to 8
Outputs:
- standardized_mixer_result: bfloat16 [2048, 4096], P(('groups', 'ctx'), 'width'), parts along dimension 0
- steered: bfloat16 [2048, 4096], P(('groups', 'ctx'), 'width'), parts along dimension 0
There are 2 independent parts, one for each index of `groups`. A program takes and returns all parts, laid end to end along the dimension named above; an argument that names none is the same for every part. Nothing has to cross between parts.
Inputs may be any that keep to these rules, and one draw needn't show every extreme that they name: `panel_holder_choice`: each tile names 2 different owners; the tiles of one device name one owner at most 8 times, and in every draw some device's tiles name some owner exactly 8 times.
All inputs are finite; a program needn't handle non-finite values. No bound on the sum of `holder_group_enabled` on one device may be relied on, other than what follows from the above.
Results may differ from a plain program's by a relative error of at most 0.015.
Values may be sent and summed in bfloat16 or wider, within the bound.
A program may use at most 128 MiB of HBM per device.

v0:
```python
import jax
import jax.numpy as jnp
from jax import lax
from jax.sharding import PartitionSpec as P

ATTN_GROUP_DIM = 64
SUB = 32
TILE = 8
BLK = 128
HIGHEST = lax.Precision.HIGHEST


def passed_along(block, axis, distance):
    devices = range(lax.axis_size(axis))
    route = [(i - distance, i) for i in devices if i - distance in devices]
    return lax.ppermute(block, axis, route)


def block_step(carried, pieces):
    rec_in, key_in, val_in, rate_in, learn_in = pieces
    length = rec_in.shape[0]
    removal = key_in * lax.rsqrt(
        jnp.sum(key_in * key_in, -1, keepdims=True) + key_in.shape[-1] * 1e-05
    )
    erase_a = -removal
    erase_b = removal * learn_in
    log_cum = -jnp.cumsum(rate_in, axis=0)
    cum_now = jnp.exp(log_cum)
    cum_prev = jnp.exp(log_cum + rate_in)
    undo = jnp.exp(-log_cum)
    left_a = erase_a * cum_prev
    left_r = rec_in * cum_now
    right_b = erase_b * undo
    right_k = key_in * undo
    row_ids = lax.broadcasted_iota(jnp.int32, (length, length), 0)
    col_ids = lax.broadcasted_iota(jnp.int32, (length, length), 1)
    strict = (row_ids > col_ids).astype(jnp.float32)
    inclusive = (row_ids >= col_ids).astype(jnp.float32)
    mix_ab = jnp.einsum("thk,jhk->htj", left_a, right_b, precision=HIGHEST) * strict
    mix_ak = jnp.einsum("thk,jhk->htj", left_a, right_k, precision=HIGHEST) * strict
    mix_rb = jnp.einsum("thk,jhk->htj", left_r, right_b, precision=HIGHEST) * inclusive
    mix_rk = jnp.einsum("thk,jhk->htj", left_r, right_k, precision=HIGHEST) * inclusive
    padded_v = jnp.concatenate([val_in, jnp.zeros_like(val_in)], -1)
    target = jnp.einsum("thk,hxk->htx", left_a, carried, precision=HIGHEST) + jnp.einsum(
        "htj,jhx->htx", mix_ak, padded_v, precision=HIGHEST
    )
    inverse = jnp.eye(length, dtype=jnp.float32)[None] + mix_ab
    power = mix_ab
    for doubling in range(length.bit_length() - 2):
        power = jnp.einsum("hij,hjk->hik", power, power, precision=HIGHEST)
        inverse = inverse + jnp.einsum("hij,hjk->hik", inverse, power, precision=HIGHEST)
    reads = jnp.einsum("htj,hjx->htx", inverse, target, precision=HIGHEST)
    outputs = (
        jnp.einsum("thk,hxk->htx", left_r, carried, precision=HIGHEST)
        + jnp.einsum("htj,hjx->htx", mix_rb, reads, precision=HIGHEST)
        + jnp.einsum("htj,jhx->htx", mix_rk, padded_v, precision=HIGHEST)
    )
    fade = cum_now[-1]
    updated = (
        carried
        + jnp.einsum("hjx,jhk->hxk", reads, right_b, precision=HIGHEST)
        + jnp.einsum("jhx,jhk->hxk", padded_v, right_k, precision=HIGHEST)
    )
    return (updated * fade[:, None, :], outputs)


def activate(preacts, mask_vals, index_vals, value_vals):
    senders, items, block_count = mask_vals.shape
    codes = jnp.maximum(preacts, 0.0).reshape(senders, items, TILE, block_count, BLK)
    within = lax.broadcasted_iota(jnp.int32, (block_count, BLK), 1)
    hit = within == index_vals[:, None]
    codes = jnp.where(hit, value_vals[:, None], codes)
    codes = codes * mask_vals.astype(jnp.float32)[:, :, None, :, None]
    return codes.reshape(senders * items * TILE, block_count * BLK).astype(jnp.bfloat16)


def body(
    gating_vectors,
    lookup_vectors,
    payload_vectors,
    forgetting_exponent,
    inline_adapt_factor,
    group_layer_scaling,
    group_layer_offset,
    present_reward_factor,
    shared_dictionary_matrix,
    sparse_code_offset,
    reconstruct_offset,
    panel_holder_choice,
    holder_group_enabled,
    fixed_feature_slot,
    fixed_feature_amount,
):
    tok_rows = gating_vectors.shape[0]
    feat_local = gating_vectors.shape[1]
    group_counting = feat_local // ATTN_GROUP_DIM
    gating_vectors_all = gating_vectors.astype(jnp.float32).reshape(
        tok_rows, group_counting, ATTN_GROUP_DIM
    )
    lookup_vectors_all = lookup_vectors.astype(jnp.float32).reshape(
        tok_rows, group_counting, ATTN_GROUP_DIM
    )
    payload_vectors_all = payload_vectors.astype(jnp.float32).reshape(
        tok_rows, group_counting, ATTN_GROUP_DIM
    )
    rate_all = forgetting_exponent.astype(jnp.float32).reshape(
        tok_rows, group_counting, ATTN_GROUP_DIM
    )
    learn_all = inline_adapt_factor.astype(jnp.float32).reshape(
        tok_rows, group_counting, ATTN_GROUP_DIM
    )
    block_count = tok_rows // SUB

    def stacked(array):
        return array.reshape(block_count, SUB, group_counting, ATTN_GROUP_DIM)

    eye_heads = jnp.broadcast_to(
        jnp.eye(ATTN_GROUP_DIM, dtype=jnp.float32), (group_counting, ATTN_GROUP_DIM, ATTN_GROUP_DIM)
    )
    zero_heads = jnp.zeros((group_counting, ATTN_GROUP_DIM, ATTN_GROUP_DIM), jnp.float32)
    start_state = jnp.concatenate([zero_heads, eye_heads], axis=1)
    final_state, block_outs = lax.scan(
        block_step,
        start_state,
        (
            stacked(gating_vectors_all),
            stacked(lookup_vectors_all),
            stacked(payload_vectors_all),
            stacked(rate_all),
            stacked(learn_all),
        ),
    )
    block_outs = block_outs.transpose(0, 2, 1, 3).reshape(
        tok_rows, group_counting, 2 * ATTN_GROUP_DIM
    )
    local_out = block_outs[:, :, :ATTN_GROUP_DIM]
    probe = block_outs[:, :, ATTN_GROUP_DIM:]
    own_state = final_state[:, :ATTN_GROUP_DIM, :]
    transfer = final_state[:, ATTN_GROUP_DIM:, :]

    def forward(counter, carry_pair):
        incoming = passed_along(carry_pair[1], "ctx", 1)
        leaving = jnp.einsum("hvj,hjk->hvk", incoming, transfer, precision=HIGHEST) + own_state
        return (incoming, leaving)

    prior = lax.fori_loop(0, lax.axis_size("ctx") - 1, forward, (zero_heads, own_state))[0]
    wkv = local_out + jnp.einsum("hvk,thk->thv", prior, probe, precision=HIGHEST)
    center = wkv - jnp.mean(wkv, -1, keepdims=True)
    spread = jnp.mean(center * center, -1, keepdims=True)
    standardized_lines = (center * lax.rsqrt(spread + 1e-05)).reshape(
        tok_rows, feat_local
    ) * group_layer_scaling + group_layer_offset
    present_reward = (
        jnp.sum(
            gating_vectors_all
            * lookup_vectors_all
            * present_reward_factor.reshape(group_counting, ATTN_GROUP_DIM),
            -1,
            keepdims=True,
        )
        * payload_vectors_all
    ).reshape(tok_rows, feat_local)
    standardized_mixer_result = (standardized_lines + present_reward).astype(jnp.bfloat16)
    enc_in = (standardized_mixer_result.astype(jnp.float32) - reconstruct_offset).astype(
        jnp.bfloat16
    )
    ctx_count = lax.axis_size("ctx")
    tile_count = tok_rows // TILE
    slot_count = panel_holder_choice.shape[1]
    blocks_own = holder_group_enabled.shape[2]
    capacity = max(2, 2 * tok_rows * slot_count // (TILE * ctx_count))
    pair_count = tile_count * slot_count
    owner_flat = panel_holder_choice.reshape(pair_count)
    owner_hot = (owner_flat[:, None] == lax.broadcasted_iota(jnp.int32, (1, ctx_count), 1)).astype(
        jnp.int32
    )
    ranks = jnp.sum((jnp.cumsum(owner_hot, axis=0) - owner_hot) * owner_hot, axis=1)
    slot_ids = owner_flat * capacity + ranks
    dispatch = (
        slot_ids[None, :] == lax.broadcasted_iota(jnp.int32, (ctx_count * capacity, 1), 0)
    ).astype(jnp.float32)
    tile_pick = (
        lax.broadcasted_iota(jnp.int32, (tile_count, pair_count), 1) // slot_count
        == lax.broadcasted_iota(jnp.int32, (tile_count, pair_count), 0)
    ).astype(jnp.float32)
    slot_tile = jnp.dot(dispatch, tile_pick.T)
    send_rows = jnp.dot(
        slot_tile.astype(jnp.bfloat16),
        enc_in.reshape(tile_count, TILE * feat_local),
        preferred_element_type=jnp.float32,
    )
    send_rows = send_rows.astype(jnp.bfloat16).reshape(ctx_count, capacity, TILE, feat_local)
    send_mask = jnp.dot(
        dispatch, holder_group_enabled.reshape(pair_count, blocks_own).astype(jnp.float32)
    )
    send_mask = send_mask.astype(jnp.bfloat16).reshape(ctx_count, capacity, blocks_own)
    got_rows = lax.all_to_all(send_rows, "ctx", split_axis=0, concat_axis=0, tiled=True)
    got_mask = lax.all_to_all(send_mask, "ctx", split_axis=0, concat_axis=0, tiled=True)
    senders = got_rows.shape[0]
    items = got_rows.shape[1]
    flat_rows = got_rows.reshape(senders * items * TILE, feat_local)
    partial_pre = lax.dot_general(
        flat_rows,
        shared_dictionary_matrix,
        (((1,), (1,)), ((), ())),
        preferred_element_type=jnp.float32,
    )
    total_pre = lax.psum(partial_pre.astype(jnp.bfloat16), "width").astype(jnp.float32)
    codes = activate(
        total_pre + sparse_code_offset, got_mask, fixed_feature_slot, fixed_feature_amount
    )
    decoded = jnp.dot(codes, shared_dictionary_matrix, preferred_element_type=jnp.float32).astype(
        jnp.bfloat16
    )
    returned = decoded.reshape(senders, items, TILE, feat_local)
    received = lax.all_to_all(returned, "ctx", split_axis=0, concat_axis=0, tiled=True)
    summed = jnp.dot(
        slot_tile.T.astype(jnp.bfloat16),
        received.reshape(ctx_count * capacity, TILE * feat_local),
        preferred_element_type=jnp.float32,
    )
    steered = (summed.reshape(tok_rows, feat_local) + reconstruct_offset).astype(jnp.bfloat16)
    return (standardized_mixer_result, steered)


def solution(mesh):
    placed = (
        P(("groups", "ctx"), "width"),
        P(("groups", "ctx"), "width"),
        P(("groups", "ctx"), "width"),
        P(("groups", "ctx"), "width"),
        P(("groups", "ctx"), "width"),
        P("width"),
        P("width"),
        P("width"),
        P("ctx", "width"),
        P("ctx"),
        P("width"),
        P(("groups", "ctx"), None),
        P(("groups", "ctx"), None, None),
        P("ctx"),
        P("ctx"),
    )
    return jax.shard_map(
        body,
        mesh=mesh,
        in_specs=placed,
        out_specs=(P(("groups", "ctx"), "width"), P(("groups", "ctx"), "width")),
        check_vma=False,
    )
```

profile of v0, /device:TPU:0, one launch (start us, length us, event | category | flops | bytes accessed | tf_op | source)
XLA Modules:
  0.0 519.1 jit_solution(18060309378639857099)
XLA Ops:
  26.0 119.1 %while.24 = (s32[]{:T(128)}, f32[32,128,64]{1,2,0:T(8,128)S(1)}, f32[4,32,32,128]{3,1,2,0:T(8,128)}, f32[4,32,32,64]{3,2,1,0:T(8,128)S(1)}, f32[4,32,32,64]{3,2,...) while((s32[]{:T(128)}, f32[32,128,64]{1,2,0:T(8,128)S(1)}, ...), condition=%wide.region_3.4_spmd, body=%wide.region_0.3_spmd.sunk | while | flops 809539584 | bytes 26289764 | solution.py:122
  149.7 4.8 fusion.64
  158.2 189.7 %while.25 = (s32[]{:T(128)}, f32[32,64,64]{2,1,0:T(8,128)}, f32[32,64,64]{2,1,0:T(8,128)}, f32[32,64,64]{2,1,0:T(8,128)S(1)}, f32[32,64,64]{2,1,0:T(8,128)S(1)}, /*index=5*/s32[]{:T(128)}) while((s32[]{:T(128)}, f32[32,64,64]{2,1,0:T(8,128)}, f32[32,64,64]{2,1,0:T(8,128)}, f32[32,64,64]{2,1,0:T(8,128)S(1)}, f32[32,64,64]{2,1,0:T(8,128)S(1)}, ...), condition=%wide.region_5.6_spmd, body=%wide.region_4.5_spmd.sunk | while | flops 100794368 | bytes 6291593 | solution.py:146
  158.2 4.9 collective-permute-start
  163.1 22.7 %collective-permute-done = f32[32,64,64]{2,1,0:T(8,128)S(1)} collective-permute-done((f32[32,64,64]{2,1,0:T(8,128)}, f32[32,64,64]{2,1,0:T(8,128)S(1)}, u32[]{:S(2)}, u32[]{:S(2)}) %collective-permute-start) | collective-permute-done | bytes 524320 | tf_op jit(solution)/shard_map/while/body/eval_jaxpr/ppermute | solution.py:16
  192.4 21.8 %collective-permute-done = f32[32,64,64]{2,1,0:T(8,128)S(1)} collective-permute-done((f32[32,64,64]{2,1,0:T(8,128)}, f32[32,64,64]{2,1,0:T(8,128)S(1)}, u32[]{:S(2)}, u32[]{:S(2)}) %collective-permute-start) | collective-permute-done | bytes 524320 | tf_op jit(solution)/shard_map/while/body/eval_jaxpr/ppermute | solution.py:16
  216.4 4.4 collective-permute-start
  220.7 20.9 %collective-permute-done = f32[32,64,64]{2,1,0:T(8,128)S(1)} collective-permute-done((f32[32,64,64]{2,1,0:T(8,128)}, f32[32,64,64]{2,1,0:T(8,128)S(1)}, u32[]{:S(2)}, u32[]{:S(2)}) %collective-permute-start) | collective-permute-done | bytes 524320 | tf_op jit(solution)/shard_map/while/body/eval_jaxpr/ppermute | solution.py:16
  243.8 5.2 %collective-permute-start = (f32[32,64,64]{2,1,0:T(8,128)}, f32[32,64,64]{2,1,0:T(8,128)S(1)}, u32[]{:S(2)}, u32[]{:S(2)}) collective-permute-start(f32[32,64,64]{2,1,0:T(8,128)} %get-tuple-element.269), channel_id=1, source_target_pairs={{0,2},{2,4},{4,6},{6,8},{8,10},{10,12},{12,14},{1,3},{3,5},{5,7},{... | collective-permute-start | bytes 1572872 | tf_op jit(solution)/shard_map/while/body/eval_jaxpr/ppermute | solution.py:16
  249.1 19.9 %collective-permute-done = f32[32,64,64]{2,1,0:T(8,128)S(1)} collective-permute-done((f32[32,64,64]{2,1,0:T(8,128)}, f32[32,64,64]{2,1,0:T(8,128)S(1)}, u32[]{:S(2)}, u32[]{:S(2)}) %collective-permute-start) | collective-permute-done | bytes 524320 | tf_op jit(solution)/shard_map/while/body/eval_jaxpr/ppermute | solution.py:16
  271.2 5.2 %collective-permute-start = (f32[32,64,64]{2,1,0:T(8,128)}, f32[32,64,64]{2,1,0:T(8,128)S(1)}, u32[]{:S(2)}, u32[]{:S(2)}) collective-permute-start(f32[32,64,64]{2,1,0:T(8,128)} %get-tuple-element.269), channel_id=1, source_target_pairs={{0,2},{2,4},{4,6},{6,8},{8,10},{10,12},{12,14},{1,3},{3,5},{5,7},{... | collective-permute-start | bytes 1572872 | tf_op jit(solution)/shard_map/while/body/eval_jaxpr/ppermute | solution.py:16
  276.5 19.0 %collective-permute-done = f32[32,64,64]{2,1,0:T(8,128)S(1)} collective-permute-done((f32[32,64,64]{2,1,0:T(8,128)}, f32[32,64,64]{2,1,0:T(8,128)S(1)}, u32[]{:S(2)}, u32[]{:S(2)}) %collective-permute-start) | collective-permute-done | bytes 524320 | tf_op jit(solution)/shard_map/while/body/eval_jaxpr/ppermute | solution.py:16
  297.7 5.2 %collective-permute-start = (f32[32,64,64]{2,1,0:T(8,128)}, f32[32,64,64]{2,1,0:T(8,128)S(1)}, u32[]{:S(2)}, u32[]{:S(2)}) collective-permute-start(f32[32,64,64]{2,1,0:T(8,128)} %get-tuple-element.269), channel_id=1, source_target_pairs={{0,2},{2,4},{4,6},{6,8},{8,10},{10,12},{12,14},{1,3},{3,5},{5,7},{... | collective-permute-start | bytes 1572872 | tf_op jit(solution)/shard_map/while/body/eval_jaxpr/ppermute | solution.py:16
  303.0 18.1 %collective-permute-done = f32[32,64,64]{2,1,0:T(8,128)S(1)} collective-permute-done((f32[32,64,64]{2,1,0:T(8,128)}, f32[32,64,64]{2,1,0:T(8,128)S(1)}, u32[]{:S(2)}, u32[]{:S(2)}) %collective-permute-start) | collective-permute-done | bytes 524320 | tf_op jit(solution)/shard_map/while/body/eval_jaxpr/ppermute | solution.py:16
  323.3 5.2 %collective-permute-start = (f32[32,64,64]{2,1,0:T(8,128)}, f32[32,64,64]{2,1,0:T(8,128)S(1)}, u32[]{:S(2)}, u32[]{:S(2)}) collective-permute-start(f32[32,64,64]{2,1,0:T(8,128)} %get-tuple-element.269), channel_id=1, source_target_pairs={{0,2},{2,4},{4,6},{6,8},{8,10},{10,12},{12,14},{1,3},{3,5},{5,7},{... | collective-permute-start | bytes 1572872 | tf_op jit(solution)/shard_map/while/body/eval_jaxpr/ppermute | solution.py:16
  328.5 17.2 %collective-permute-done = f32[32,64,64]{2,1,0:T(8,128)S(1)} collective-permute-done((f32[32,64,64]{2,1,0:T(8,128)}, f32[32,64,64]{2,1,0:T(8,128)S(1)}, u32[]{:S(2)}, u32[]{:S(2)}) %collective-permute-start) | collective-permute-done | bytes 524320 | tf_op jit(solution)/shard_map/while/body/eval_jaxpr/ppermute | solution.py:16
  347.9 7.0 %fusion.66 = (f32[128,32]{0,1:T(8,128)S(1)}, f32[128,32,64]{0,2,1:T(8,128)S(1)}) fusion(f32[128,32,64]{0,2,1:T(8,128)} %copy.85, f32[32,64,64]{2,1,0:T(8,128)} %get-tuple-element.73, f32[128,32,64]{2,1,0:T(8,128)} %get-tuple-element.138), kind=kOutput, calls=%fused_computation.118 | convolution fusion | flops 201846784 | bytes 3686400 | tf_op jit(solution)/shard_map/hvk,thk->thv/dot_general | solution.py:147
  363.4 50.3 %all_to_all.15 = bf16[8,8,8,2048]{3,2,1,0:T(8,128)(2,1)S(1)} all-to-all(bf16[8,8,8,2048]{3,2,1,0:T(8,128)(2,1)S(1)} %copy.77), channel_id=1, replica_groups=mesh['groups'=2,'ctx'=8,'width'=2] {'ctx'}, dimensions={0} | all-to-all | bytes 4194304 | tf_op jit(solution)/shard_map/all_to_all | solution.py:197
  413.7 9.1 %convolution_convert_fusion.2 = bf16[512,2048]{1,0:T(8,128)(2,1)} fusion(bf16[512,2048]{1,0:T(8,128)(2,1)S(1)} %bitcast.176, bf16[2048,2048]{1,0:T(8,128)(2,1)} %param.27), kind=kOutput, calls=%fused_computation.68 | convolution fusion | flops 4296015872 | bytes 12582912 | tf_op jit(solution)/shard_map/dot_general | solution.py:202
  428.2 6.4 %all-to-all-done.1 = bf16[8,8,16]{2,1,0:T(8,128)(2,1)S(1)} async-done(((bf16[8,8,16]{2,1,0:T(8,128)(2,1)}), bf16[8,8,16]{2,1,0:T(8,128)(2,1)S(1)}, u32[]{:S(2)}, u32[]{:S(2)}) %all-to-all-start.1) | async-done | bytes 2080 | tf_op jit(solution)/shard_map/all_to_all | solution.py:198
  434.6 8.6 %all-reduce.4.cloned.1.call-done = bf16[512,2048]{1,0:T(8,128)(2,1)} async-done(((bf16[512,2048]{1,0:T(8,128)(2,1)}), bf16[512,2048]{1,0:T(8,128)(2,1)}) %all-reduce.4.cloned.1.call-update) | async-done | bytes 2097168 | tf_op jit(solution)/shard_map/psum | solution.py:208
  444.9 9.2 %convolution_convert_fusion.1 = bf16[512,2048]{1,0:T(8,128)(2,1)} fusion(bf16[2048,2048]{1,0:T(8,128)(2,1)} %param.27, f32[512,2048]{1,0:T(8,128)S(1)} %bitcast.173, bf16[512,2048]{1,0:T(8,128)(2,1)S(1)} %copy-done.15, f32[2048]{0:T(1024)S(1)} %copy-done.16, f32[2048]{0:T(1024)S(1)} %broadcast_bitcast_fusion, pred[2048]{0:T(1024)(128)(4,1)S(1)} %fusion.58), kind=kOutput, calls=%fused_computation.67 | convolution fusion | flops 4302307328 | bytes 16795648 | tf_op jit(solution)/shard_map/dot_general | solution.py:212
  454.1 5.8 %all-to-all-start.2 = ((bf16[8,8,8,2048]{3,2,1,0:T(8,128)(2,1)}), bf16[8,8,8,2048]{3,2,1,0:T(8,128)(2,1)S(1)}, u32[]{:S(2)}, u32[]{:S(2)}) async-start(bf16[8,8,8,2048]{3,2,1,0:T(8,128)(2,1)} %bitcast.175), calls=%async_computation.2 | async-start | bytes 4194304 | tf_op jit(solution)/shard_map/all_to_all | solution.py:216
  460.9 47.7 %all-to-all-done.2 = bf16[8,8,8,2048]{3,2,1,0:T(8,128)(2,1)S(1)} async-done(((bf16[8,8,8,2048]{3,2,1,0:T(8,128)(2,1)}), bf16[8,8,8,2048]{3,2,1,0:T(8,128)(2,1)S(1)}, u32[]{:S(2)}, u32[]{:S(2)}) %all-to-all-start.2) | async-done | bytes 2097184 | tf_op jit(solution)/shard_map/all_to_all | solution.py:216
  (231 shorter events, 169.7 us)
Async XLA Ops:
  7.2 420.9 %copy-start = (f32[16]{0:T(128)S(1)}, f32[16]{0:T(128)}, u32[]{:S(2)}) copy-start(f32[16]{0:T(128)} %param.33) | copy-start | bytes 196
  7.2 436.1 %all-reduce.4.cloned.1.call-start = ((), (), s32[]{:S(2)}) async-start(), calls=%async_computation.3 | async-start | bytes 4194304 | tf_op jit(solution)/shard_map/psum | solution.py:208
  13.6 4.3 copy-start.2
  17.9 3.1 copy-start.5
  21.0 2.3 copy-start.6
  158.2 27.6 %collective-permute-start = (f32[32,64,64]{2,1,0:T(8,128)}, f32[32,64,64]{2,1,0:T(8,128)S(1)}, u32[]{:S(2)}, u32[]{:S(2)}) collective-permute-start(f32[32,64,64]{2,1,0:T(8,128)} %get-tuple-element.269), channel_id=1, source_target_pairs={{0,2},{2,4},{4,6},{6,8},{8,10},{10,12},{12,14},{1,3},{3,5},{5,7},{... | collective-permute-start | bytes 1572872 | tf_op jit(solution)/shard_map/while/body/eval_jaxpr/ppermute | solution.py:16
  185.8 2.2 copy-start.1
  188.0 26.1 %collective-permute-start = (f32[32,64,64]{2,1,0:T(8,128)}, f32[32,64,64]{2,1,0:T(8,128)S(1)}, u32[]{:S(2)}, u32[]{:S(2)}) collective-permute-start(f32[32,64,64]{2,1,0:T(8,128)} %get-tuple-element.269), channel_id=1, source_target_pairs={{0,2},{2,4},{4,6},{6,8},{8,10},{10,12},{12,14},{1,3},{3,5},{5,7},{... | collective-permute-start | bytes 1572872 | tf_op jit(solution)/shard_map/while/body/eval_jaxpr/ppermute | solution.py:16
  216.4 25.2 %collective-permute-start = (f32[32,64,64]{2,1,0:T(8,128)}, f32[32,64,64]{2,1,0:T(8,128)S(1)}, u32[]{:S(2)}, u32[]{:S(2)}) collective-permute-start(f32[32,64,64]{2,1,0:T(8,128)} %get-tuple-element.269), channel_id=1, source_target_pairs={{0,2},{2,4},{4,6},{6,8},{8,10},{10,12},{12,14},{1,3},{3,5},{5,7},{... | collective-permute-start | bytes 1572872 | tf_op jit(solution)/shard_map/while/body/eval_jaxpr/ppermute | solution.py:16
  241.6 2.2 copy-start.1
  243.8 25.2 %collective-permute-start = (f32[32,64,64]{2,1,0:T(8,128)}, f32[32,64,64]{2,1,0:T(8,128)S(1)}, u32[]{:S(2)}, u32[]{:S(2)}) collective-permute-start(f32[32,64,64]{2,1,0:T(8,128)} %get-tuple-element.269), channel_id=1, source_target_pairs={{0,2},{2,4},{4,6},{6,8},{8,10},{10,12},{12,14},{1,3},{3,5},{5,7},{... | collective-permute-start | bytes 1572872 | tf_op jit(solution)/shard_map/while/body/eval_jaxpr/ppermute | solution.py:16
  269.0 2.2 copy-start.1
  271.2 24.2 %collective-permute-start = (f32[32,64,64]{2,1,0:T(8,128)}, f32[32,64,64]{2,1,0:T(8,128)S(1)}, u32[]{:S(2)}, u32[]{:S(2)}) collective-permute-start(f32[32,64,64]{2,1,0:T(8,128)} %get-tuple-element.269), channel_id=1, source_target_pairs={{0,2},{2,4},{4,6},{6,8},{8,10},{10,12},{12,14},{1,3},{3,5},{5,7},{... | collective-permute-start | bytes 1572872 | tf_op jit(solution)/shard_map/while/body/eval_jaxpr/ppermute | solution.py:16
  297.7 23.3 %collective-permute-start = (f32[32,64,64]{2,1,0:T(8,128)}, f32[32,64,64]{2,1,0:T(8,128)S(1)}, u32[]{:S(2)}, u32[]{:S(2)}) collective-permute-start(f32[32,64,64]{2,1,0:T(8,128)} %get-tuple-element.269), channel_id=1, source_target_pairs={{0,2},{2,4},{4,6},{6,8},{8,10},{10,12},{12,14},{1,3},{3,5},{5,7},{... | collective-permute-start | bytes 1572872 | tf_op jit(solution)/shard_map/while/body/eval_jaxpr/ppermute | solution.py:16
  323.3 22.4 %collective-permute-start = (f32[32,64,64]{2,1,0:T(8,128)}, f32[32,64,64]{2,1,0:T(8,128)S(1)}, u32[]{:S(2)}, u32[]{:S(2)}) collective-permute-start(f32[32,64,64]{2,1,0:T(8,128)} %get-tuple-element.269), channel_id=1, source_target_pairs={{0,2},{2,4},{4,6},{6,8},{8,10},{10,12},{12,14},{1,3},{3,5},{5,7},{... | collective-permute-start | bytes 1572872 | tf_op jit(solution)/shard_map/while/body/eval_jaxpr/ppermute | solution.py:16
  345.7 2.2 copy-start.1
  355.1 3.9 copy-start.3
  355.1 3.9 copy-start.8
  355.1 3.9 copy-start.10
  355.1 3.9 copy-start.11
  422.8 5.3 %copy-start.14 = (s32[16]{0:T(128)S(1)}, s32[16]{0:T(128)}, u32[]{:S(2)}) copy-start(s32[16]{0:T(128)} %param.32) | copy-start | bytes 196
  424.4 10.2 %all-to-all-start.1 = ((bf16[8,8,16]{2,1,0:T(8,128)(2,1)}), bf16[8,8,16]{2,1,0:T(8,128)(2,1)S(1)}, u32[]{:S(2)}, u32[]{:S(2)}) async-start(bf16[8,8,16]{2,1,0:T(8,128)(2,1)} %bitcast.19), calls=%async_computation.1 | async-start | bytes 32768 | tf_op jit(solution)/shard_map/all_to_all | solution.py:198
  428.2 16.2 %copy-start.16 = (f32[2048]{0:T(1024)S(1)}, f32[2048]{0:T(1024)}, u32[]{:S(2)}) copy-start(f32[2048]{0:T(1024)} %param.28) | copy-start | bytes 24580
  454.1 54.5 %all-to-all-start.2 = ((bf16[8,8,8,2048]{3,2,1,0:T(8,128)(2,1)}), bf16[8,8,8,2048]{3,2,1,0:T(8,128)(2,1)S(1)}, u32[]{:S(2)}, u32[]{:S(2)}) async-start(bf16[8,8,8,2048]{3,2,1,0:T(8,128)(2,1)} %bitcast.175), calls=%async_computation.2 | async-start | bytes 4194304 | tf_op jit(solution)/shard_map/all_to_all | solution.py:216
  (9 other events, 14.3 us)
Sparse Core Ops, SparseCore 0:
  423.0 20.2 all-reduce.3
where the time goes:
time: 525 us; the launch traced here: 519 us
  waiting for transfers between devices  202 us (38%)
  matrix products  127 us (24%)
  local copies, waits for them, and re-layouts  50.3 us (10%)
  blocking collectives  50.3 us (10%)
  starting transfers between devices  44 us (8%)
  loops' own time  16.2 us (3%)
  other arithmetic  15 us (3%)
  between operations  14.6 us (3%)
    ppermute x7, waiting for transfers between devices, passed_along(): return lax.ppermute(block, axis, route)  139 us
    all_to_all x1, blocking collectives, body(): lax.all_to_all(send_rows, 'ctx', split_axis=0, concat_axis=0, tiled=True)  50.3 us
    all_to_all x1, waiting for transfers between devices, body(): lax.all_to_all(returned, 'ctx', split_axis=0, concat_axis=0, tiled=True)  47.7 us
    ppermute x7, starting transfers between devices, passed_along(): return lax.ppermute(block, axis, route)  34.6 us
    another operation x1, loops' own time, body(): lax.scan(block_step, start_state, (stacked(gating_vectors_all), stacked(l...  16.1 us
    dot_general x7, matrix products, forward(): jnp.einsum('hvj,hjk->hvk', incoming, transfer, precision=HIGHEST)  15.6 us
    unnamed x41, local copies, waits for them, and re-layouts  12.8 us
    another operation x5, local copies, waits for them, and re-layouts, stacked(): return array.reshape(block_count, SUB, group_counting, ATTN_GROUP_DIM)  11.5 us
  transfers between devices with their start and end apart: 10, of which 10 were waited for; matrix products, arithmetic and copies ran while one was open for 0% of the time, Pallas kernels for 0%

commit v1 on v0

--- a/solution.py
+++ b/solution.py
@@ -8,6 +8,22 @@
 TILE = 8
 BLK = 128
 HIGHEST = lax.Precision.HIGHEST
+
+
+def swapped_with_each(x, axis, split, join):
+    ways, here = (lax.axis_size(axis), lax.axis_index(axis))
+    width = x.shape[split] // ways
+    shape = list(x.shape)
+    shape[split] = width
+    height = shape[join]
+    shape[join] = height * ways
+    full = jnp.zeros(shape, x.dtype)
+    for mask in range(ways):
+        part = lax.dynamic_slice_in_dim(x, (here ^ mask) * width, width, axis=split)
+        if mask:
+            part = lax.ppermute(part, axis, [(d, d ^ mask) for d in range(ways)])
+        full = lax.dynamic_update_slice_in_dim(full, part, (here ^ mask) * height, axis=join)
+    return full
 
 
 def passed_along(block, axis, distance):
@@ -194,7 +210,7 @@
         dispatch, holder_group_enabled.reshape(pair_count, blocks_own).astype(jnp.float32)
     )
     send_mask = send_mask.astype(jnp.bfloat16).reshape(ctx_count, capacity, blocks_own)
-    got_rows = lax.all_to_all(send_rows, "ctx", split_axis=0, concat_axis=0, tiled=True)
+    got_rows = swapped_with_each(send_rows, "ctx", 0, 0)
     got_mask = lax.all_to_all(send_mask, "ctx", split_axis=0, concat_axis=0, tiled=True)
     senders = got_rows.shape[0]
     items = got_rows.shape[1]

time: 525 us -> 524 us (level)
  blocking collectives: 50.3 us -> 0 us
  starting transfers between devices: 44 us -> 71.1 us
  waiting for transfers between devices: 202 us -> 224 us
    all_to_all x1 -> x0, blocking collectives: 50.3 us -> none  [body(): lax.all_to_all(send_rows, 'ctx', split_axis=0, concat_axis=0, tiled=True)]
    ppermute x0 -> x7, waiting for transfers between devices: none -> 21.5 us  [swapped_with_each(): part = lax.ppermute(part, axis, [(d, d ^ mask) for d in range(ways)])]
    ppermute x0 -> x7, starting transfers between devices: none -> 20 us  [swapped_with_each(): part = lax.ppermute(part, axis, [(d, d ^ mask) for d in range(ways)])]
    all_to_all x1, starting transfers between devices: 3.6 us -> 10.8 us  [body(): lax.all_to_all(send_mask, 'ctx', split_axis=0, concat_axis=0, tiled=True)]
    unnamed x41 -> x48, local copies, waits for them, and re-layouts: 12.8 us -> 13.9 us
  transfers between devices with their start and end apart: 10 -> 17, of which waited for: 10 -> 13; matrix products, arithmetic and copies ran while one was open for 0% -> 1% of each run, Pallas kernels for 0% -> 0%
where the time goes in v1:
time: 524 us; the launch traced here: 519 us
  waiting for transfers between devices  224 us (43%)
  matrix products  127 us (24%)
  starting transfers between devices  71.1 us (14%)
  local copies, waits for them, and re-layouts  51 us (10%)
  loops' own time  16.2 us (3%)
  other arithmetic  15.2 us (3%)
  between operations  14.8 us (3%)
    ppermute x7, waiting for transfers between devices, passed_along(): return lax.ppermute(block, axis, route)  139 us
    all_to_all x1, waiting for transfers between devices, body(): lax.all_to_all(returned, 'ctx', split_axis=0, concat_axis=0, tiled=True)  47.7 us
    ppermute x7, starting transfers between devices, passed_along(): return lax.ppermute(block, axis, route)  34.6 us
    ppermute x7, waiting for transfers between devices, swapped_with_each(): part = lax.ppermute(part, axis, [(d, d ^ mask) for d in range(ways)])  21.5 us
    ppermute x7, starting transfers between devices, swapped_with_each(): part = lax.ppermute(part, axis, [(d, d ^ mask) for d in range(ways)])  20 us
    another operation x1, loops' own time, body(): lax.scan(block_step, start_state, (stacked(gating_vectors_all), stacked(l...  16.1 us
    dot_general x7, matrix products, forward(): jnp.einsum('hvj,hjk->hvk', incoming, transfer, precision=HIGHEST)  15.6 us
    unnamed x48, local copies, waits for them, and re-layouts  13.9 us
  transfers between devices with their start and end apart: 17, of which 13 were waited for; matrix products, arithmetic and copies ran while one was open for 1% of the time, Pallas kernels for 0%

profile of v1, /device:TPU:0, one launch (start us, length us, event | category | flops | bytes accessed | tf_op | source)
XLA Modules:
  0.0 518.5 jit_solution(10789600529413978075)
XLA Ops:
  26.1 119.1 %while.24 = (s32[]{:T(128)}, f32[32,128,64]{1,2,0:T(8,128)S(1)}, f32[4,32,32,128]{3,1,2,0:T(8,128)}, f32[4,32,32,64]{3,2,1,0:T(8,128)S(1)}, f32[4,32,32,64]{3,2,...) while((s32[]{:T(128)}, f32[32,128,64]{1,2,0:T(8,128)S(1)}, ...), condition=%wide.region_3.4_spmd, body=%wide.region_0.3_spmd.sunk | while | flops 809539584 | bytes 26289764 | solution.py:138
  158.3 189.7 %while.25 = (s32[]{:T(128)}, f32[32,64,64]{2,1,0:T(8,128)}, f32[32,64,64]{2,1,0:T(8,128)}, f32[32,64,64]{2,1,0:T(8,128)S(1)}, f32[32,64,64]{2,1,0:T(8,128)S(1)}, /*index=5*/s32[]{:T(128)}) while((s32[]{:T(128)}, f32[32,64,64]{2,1,0:T(8,128)}, f32[32,64,64]{2,1,0:T(8,128)}, f32[32,64,64]{2,1,0:T(8,128)S(1)}, f32[32,64,64]{2,1,0:T(8,128)S(1)}, ...), condition=%wide.region_5.6_spmd, body=%wide.region_4.5_spmd.sunk | while | flops 100794368 | bytes 6291593 | solution.py:162
  163.3 22.7 %collective-permute-done = f32[32,64,64]{2,1,0:T(8,128)S(1)} collective-permute-done((f32[32,64,64]{2,1,0:T(8,128)}, f32[32,64,64]{2,1,0:T(8,128)S(1)}, u32[]{:S(2)}, u32[]{:S(2)}) %collective-permute-start) | collective-permute-done | bytes 524320 | tf_op jit(solution)/shard_map/while/body/eval_jaxpr/ppermute | solution.py:32
  192.5 21.8 %collective-permute-done = f32[32,64,64]{2,1,0:T(8,128)S(1)} collective-permute-done((f32[32,64,64]{2,1,0:T(8,128)}, f32[32,64,64]{2,1,0:T(8,128)S(1)}, u32[]{:S(2)}, u32[]{:S(2)}) %collective-permute-start) | collective-permute-done | bytes 524320 | tf_op jit(solution)/shard_map/while/body/eval_jaxpr/ppermute | solution.py:32
  220.9 20.9 %collective-permute-done = f32[32,64,64]{2,1,0:T(8,128)S(1)} collective-permute-done((f32[32,64,64]{2,1,0:T(8,128)}, f32[32,64,64]{2,1,0:T(8,128)S(1)}, u32[]{:S(2)}, u32[]{:S(2)}) %collective-permute-start) | collective-permute-done | bytes 524320 | tf_op jit(solution)/shard_map/while/body/eval_jaxpr/ppermute | solution.py:32
  244.0 5.2 %collective-permute-start = (f32[32,64,64]{2,1,0:T(8,128)}, f32[32,64,64]{2,1,0:T(8,128)S(1)}, u32[]{:S(2)}, u32[]{:S(2)}) collective-permute-start(f32[32,64,64]{2,1,0:T(8,128)} %get-tuple-element.277), channel_id=1, source_target_pairs={{0,2},{2,4},{4,6},{6,8},{8,10},{10,12},{12,14},{1,3},{3,5},{5,7},{... | collective-permute-start | bytes 1572872 | tf_op jit(solution)/shard_map/while/body/eval_jaxpr/ppermute | solution.py:32
  249.2 19.9 %collective-permute-done = f32[32,64,64]{2,1,0:T(8,128)S(1)} collective-permute-done((f32[32,64,64]{2,1,0:T(8,128)}, f32[32,64,64]{2,1,0:T(8,128)S(1)}, u32[]{:S(2)}, u32[]{:S(2)}) %collective-permute-start) | collective-permute-done | bytes 524320 | tf_op jit(solution)/shard_map/while/body/eval_jaxpr/ppermute | solution.py:32
  271.4 5.2 %collective-permute-start = (f32[32,64,64]{2,1,0:T(8,128)}, f32[32,64,64]{2,1,0:T(8,128)S(1)}, u32[]{:S(2)}, u32[]{:S(2)}) collective-permute-start(f32[32,64,64]{2,1,0:T(8,128)} %get-tuple-element.277), channel_id=1, source_target_pairs={{0,2},{2,4},{4,6},{6,8},{8,10},{10,12},{12,14},{1,3},{3,5},{5,7},{... | collective-permute-start | bytes 1572872 | tf_op jit(solution)/shard_map/while/body/eval_jaxpr/ppermute | solution.py:32
  276.6 19.0 %collective-permute-done = f32[32,64,64]{2,1,0:T(8,128)S(1)} collective-permute-done((f32[32,64,64]{2,1,0:T(8,128)}, f32[32,64,64]{2,1,0:T(8,128)S(1)}, u32[]{:S(2)}, u32[]{:S(2)}) %collective-permute-start) | collective-permute-done | bytes 524320 | tf_op jit(solution)/shard_map/while/body/eval_jaxpr/ppermute | solution.py:32
  297.9 5.2 %collective-permute-start = (f32[32,64,64]{2,1,0:T(8,128)}, f32[32,64,64]{2,1,0:T(8,128)S(1)}, u32[]{:S(2)}, u32[]{:S(2)}) collective-permute-start(f32[32,64,64]{2,1,0:T(8,128)} %get-tuple-element.277), channel_id=1, source_target_pairs={{0,2},{2,4},{4,6},{6,8},{8,10},{10,12},{12,14},{1,3},{3,5},{5,7},{... | collective-permute-start | bytes 1572872 | tf_op jit(solution)/shard_map/while/body/eval_jaxpr/ppermute | solution.py:32
  303.1 18.1 %collective-permute-done = f32[32,64,64]{2,1,0:T(8,128)S(1)} collective-permute-done((f32[32,64,64]{2,1,0:T(8,128)}, f32[32,64,64]{2,1,0:T(8,128)S(1)}, u32[]{:S(2)}, u32[]{:S(2)}) %collective-permute-start) | collective-permute-done | bytes 524320 | tf_op jit(solution)/shard_map/while/body/eval_jaxpr/ppermute | solution.py:32
  323.4 5.2 %collective-permute-start = (f32[32,64,64]{2,1,0:T(8,128)}, f32[32,64,64]{2,1,0:T(8,128)S(1)}, u32[]{:S(2)}, u32[]{:S(2)}) collective-permute-start(f32[32,64,64]{2,1,0:T(8,128)} %get-tuple-element.277), channel_id=1, source_target_pairs={{0,2},{2,4},{4,6},{6,8},{8,10},{10,12},{12,14},{1,3},{3,5},{5,7},{... | collective-permute-start | bytes 1572872 | tf_op jit(solution)/shard_map/while/body/eval_jaxpr/ppermute | solution.py:32
  328.7 17.2 %collective-permute-done = f32[32,64,64]{2,1,0:T(8,128)S(1)} collective-permute-done((f32[32,64,64]{2,1,0:T(8,128)}, f32[32,64,64]{2,1,0:T(8,128)S(1)}, u32[]{:S(2)}, u32[]{:S(2)}) %collective-permute-start) | collective-permute-done | bytes 524320 | tf_op jit(solution)/shard_map/while/body/eval_jaxpr/ppermute | solution.py:32
  348.1 7.0 %fusion.66 = (f32[128,32]{0,1:T(8,128)S(1)}, f32[128,32,64]{0,2,1:T(8,128)S(1)}) fusion(f32[128,32,64]{0,2,1:T(8,128)} %copy.99, f32[32,64,64]{2,1,0:T(8,128)} %get-tuple-element.73, f32[128,32,64]{2,1,0:T(8,128)} %get-tuple-element.146), kind=kOutput, calls=%fused_computation.134 | convolution fusion | flops 201846784 | bytes 3686400 | tf_op jit(solution)/shard_map/hvk,thk->thv/dot_general | solution.py:163
  374.3 6.8 %collective-permute-start.6 = (bf16[1,8,8,2048]{3,2,1,0:T(8,128)(2,1)S(1)}, bf16[1,8,8,2048]{3,2,1,0:T(8,128)(2,1)S(1)}, u32[]{:S(2)}, u32[]{:S(2)}) collective-permute-start(bf16[1,8,8,2048]{3,2,1,0:T(8,128)(2,1)S(1)} %copy.107), channel_id=1, source_target_pairs={{0,12},{2,14},{4,8},{6,10},{8,4},{10,6},{12,0},{14,2},{1,13},{3,15... | collective-permute-start | bytes 786440 | tf_op jit(solution)/shard_map/ppermute | solution.py:24
  385.9 14.0 %collective-permute-done.4 = bf16[1,8,8,2048]{3,2,1,0:T(8,128)(2,1)S(1)} collective-permute-done((bf16[1,8,8,2048]{3,2,1,0:T(8,128)(2,1)S(1)}, bf16[1,8,8,2048]{3,2,1,0:T(8,128)(2,1)S(1)}, u32[]{:S(2)}, u32[]{:S(2)}) %collective-permute-start.4) | collective-permute-done | bytes 262176 | tf_op jit(solution)/shard_map/ppermute | solution.py:24
  399.9 6.0 %collective-permute-done.5 = bf16[1,8,8,2048]{3,2,1,0:T(8,128)(2,1)S(1)} collective-permute-done((bf16[1,8,8,2048]{3,2,1,0:T(8,128)(2,1)S(1)}, bf16[1,8,8,2048]{3,2,1,0:T(8,128)(2,1)S(1)}, u32[]{:S(2)}, u32[]{:S(2)}) %collective-permute-start.5) | collective-permute-done | bytes 262176 | tf_op jit(solution)/shard_map/ppermute | solution.py:24
  406.0 9.1 %convolution_convert_fusion.2 = bf16[512,2048]{1,0:T(8,128)(2,1)} fusion(bf16[512,2048]{1,0:T(8,128)(2,1)S(1)} %bitcast.175, bf16[2048,2048]{1,0:T(8,128)(2,1)} %param.27), kind=kOutput, calls=%fused_computation.68 | convolution fusion | flops 4296015872 | bytes 12582912 | tf_op jit(solution)/shard_map/dot_general | solution.py:218
  416.7 10.8 %all-to-all-start = ((bf16[8,8,16]{2,1,0:T(8,128)(2,1)}), bf16[8,8,16]{2,1,0:T(8,128)(2,1)S(1)}, u32[]{:S(2)}, u32[]{:S(2)}) async-start(bf16[8,8,16]{2,1,0:T(8,128)(2,1)} %bitcast.19), calls=%async_computation | async-start | bytes 32768 | tf_op jit(solution)/shard_map/all_to_all | solution.py:214
  427.7 6.4 %all-to-all-done = bf16[8,8,16]{2,1,0:T(8,128)(2,1)S(1)} async-done(((bf16[8,8,16]{2,1,0:T(8,128)(2,1)}), bf16[8,8,16]{2,1,0:T(8,128)(2,1)S(1)}, u32[]{:S(2)}, u32[]{:S(2)}) %all-to-all-start) | async-done | bytes 2080 | tf_op jit(solution)/shard_map/all_to_all | solution.py:214
  434.1 8.7 %all-reduce.4.cloned.1.call-done = bf16[512,2048]{1,0:T(8,128)(2,1)} async-done(((bf16[512,2048]{1,0:T(8,128)(2,1)}), bf16[512,2048]{1,0:T(8,128)(2,1)}) %all-reduce.4.cloned.1.call-update) | async-done | bytes 2097168 | tf_op jit(solution)/shard_map/psum | solution.py:224
  444.3 9.2 %convolution_convert_fusion.1 = bf16[512,2048]{1,0:T(8,128)(2,1)} fusion(bf16[2048,2048]{1,0:T(8,128)(2,1)} %param.27, f32[512,2048]{1,0:T(8,128)S(1)} %bitcast.173, bf16[512,2048]{1,0:T(8,128)(2,1)S(1)} %copy-done.15, f32[2048]{0:T(1024)S(1)} %copy-done.16, f32[2048]{0:T(1024)S(1)} %broadcast_bitcast_fusion, pred[2048]{0:T(1024)(128)(4,1)S(1)} %fusion.58), kind=kOutput, calls=%fused_computation.67 | convolution fusion | flops 4302307328 | bytes 16795648 | tf_op jit(solution)/shard_map/dot_general | solution.py:228
  453.5 5.8 %all-to-all-start.1 = ((bf16[8,8,8,2048]{3,2,1,0:T(8,128)(2,1)}), bf16[8,8,8,2048]{3,2,1,0:T(8,128)(2,1)S(1)}, u32[]{:S(2)}, u32[]{:S(2)}) async-start(bf16[8,8,8,2048]{3,2,1,0:T(8,128)(2,1)} %bitcast.176), calls=%async_computation.1 | async-start | bytes 4194304 | tf_op jit(solution)/shard_map/all_to_all | solution.py:232
  460.3 47.7 %all-to-all-done.1 = bf16[8,8,8,2048]{3,2,1,0:T(8,128)(2,1)S(1)} async-done(((bf16[8,8,8,2048]{3,2,1,0:T(8,128)(2,1)}), bf16[8,8,8,2048]{3,2,1,0:T(8,128)(2,1)S(1)}, u32[]{:S(2)}, u32[]{:S(2)}) %all-to-all-start.1) | async-done | bytes 2097184 | tf_op jit(solution)/shard_map/all_to_all | solution.py:232
  (260 shorter events, 195.8 us)
Async XLA Ops:
  7.2 420.3 %copy-start = (f32[16]{0:T(128)S(1)}, f32[16]{0:T(128)}, u32[]{:S(2)}) copy-start(f32[16]{0:T(128)} %param.33) | copy-start | bytes 196
  7.2 435.5 %all-reduce.4.cloned.1.call-start = ((), (), s32[]{:S(2)}) async-start(), calls=%async_computation.2 | async-start | bytes 4194304 | tf_op jit(solution)/shard_map/psum | solution.py:224
  13.7 4.2 copy-start.2
  158.3 27.6 %collective-permute-start = (f32[32,64,64]{2,1,0:T(8,128)}, f32[32,64,64]{2,1,0:T(8,128)S(1)}, u32[]{:S(2)}, u32[]{:S(2)}) collective-permute-start(f32[32,64,64]{2,1,0:T(8,128)} %get-tuple-element.277), channel_id=1, source_target_pairs={{0,2},{2,4},{4,6},{6,8},{8,10},{10,12},{12,14},{1,3},{3,5},{5,7},{... | collective-permute-start | bytes 1572872 | tf_op jit(solution)/shard_map/while/body/eval_jaxpr/ppermute | solution.py:32
  188.2 26.1 %collective-permute-start = (f32[32,64,64]{2,1,0:T(8,128)}, f32[32,64,64]{2,1,0:T(8,128)S(1)}, u32[]{:S(2)}, u32[]{:S(2)}) collective-permute-start(f32[32,64,64]{2,1,0:T(8,128)} %get-tuple-element.277), channel_id=1, source_target_pairs={{0,2},{2,4},{4,6},{6,8},{8,10},{10,12},{12,14},{1,3},{3,5},{5,7},{... | collective-permute-start | bytes 1572872 | tf_op jit(solution)/shard_map/while/body/eval_jaxpr/ppermute | solution.py:32
  216.5 25.2 %collective-permute-start = (f32[32,64,64]{2,1,0:T(8,128)}, f32[32,64,64]{2,1,0:T(8,128)S(1)}, u32[]{:S(2)}, u32[]{:S(2)}) collective-permute-start(f32[32,64,64]{2,1,0:T(8,128)} %get-tuple-element.277), channel_id=1, source_target_pairs={{0,2},{2,4},{4,6},{6,8},{8,10},{10,12},{12,14},{1,3},{3,5},{5,7},{... | collective-permute-start | bytes 1572872 | tf_op jit(solution)/shard_map/while/body/eval_jaxpr/ppermute | solution.py:32
  244.0 25.2 %collective-permute-start = (f32[32,64,64]{2,1,0:T(8,128)}, f32[32,64,64]{2,1,0:T(8,128)S(1)}, u32[]{:S(2)}, u32[]{:S(2)}) collective-permute-start(f32[32,64,64]{2,1,0:T(8,128)} %get-tuple-element.277), channel_id=1, source_target_pairs={{0,2},{2,4},{4,6},{6,8},{8,10},{10,12},{12,14},{1,3},{3,5},{5,7},{... | collective-permute-start | bytes 1572872 | tf_op jit(solution)/shard_map/while/body/eval_jaxpr/ppermute | solution.py:32
  271.4 24.2 %collective-permute-start = (f32[32,64,64]{2,1,0:T(8,128)}, f32[32,64,64]{2,1,0:T(8,128)S(1)}, u32[]{:S(2)}, u32[]{:S(2)}) collective-permute-start(f32[32,64,64]{2,1,0:T(8,128)} %get-tuple-element.277), channel_id=1, source_target_pairs={{0,2},{2,4},{4,6},{6,8},{8,10},{10,12},{12,14},{1,3},{3,5},{5,7},{... | collective-permute-start | bytes 1572872 | tf_op jit(solution)/shard_map/while/body/eval_jaxpr/ppermute | solution.py:32
  297.9 23.3 %collective-permute-start = (f32[32,64,64]{2,1,0:T(8,128)}, f32[32,64,64]{2,1,0:T(8,128)S(1)}, u32[]{:S(2)}, u32[]{:S(2)}) collective-permute-start(f32[32,64,64]{2,1,0:T(8,128)} %get-tuple-element.277), channel_id=1, source_target_pairs={{0,2},{2,4},{4,6},{6,8},{8,10},{10,12},{12,14},{1,3},{3,5},{5,7},{... | collective-permute-start | bytes 1572872 | tf_op jit(solution)/shard_map/while/body/eval_jaxpr/ppermute | solution.py:32
  323.4 22.4 %collective-permute-start = (f32[32,64,64]{2,1,0:T(8,128)}, f32[32,64,64]{2,1,0:T(8,128)S(1)}, u32[]{:S(2)}, u32[]{:S(2)}) collective-permute-start(f32[32,64,64]{2,1,0:T(8,128)} %get-tuple-element.277), channel_id=1, source_target_pairs={{0,2},{2,4},{4,6},{6,8},{8,10},{10,12},{12,14},{1,3},{3,5},{5,7},{... | collective-permute-start | bytes 1572872 | tf_op jit(solution)/shard_map/while/body/eval_jaxpr/ppermute | solution.py:32
  355.3 3.9 copy-start.3
  355.3 3.9 copy-start.8
  355.3 3.9 copy-start.10
  363.0 11.3 %collective-permute-start.1 = (bf16[1,8,8,2048]{3,2,1,0:T(8,128)(2,1)S(1)}, bf16[1,8,8,2048]{3,2,1,0:T(8,128)(2,1)S(1)}, u32[]{:S(2)}, u32[]{:S(2)}) collective-permute-start(bf16[1,8,8,2048]{3,2,1,0:T(8,128)(2,1)S(1)} %copy.102), channel_id=1, source_target_pairs={{0,2},{2,0},{4,6},{6,4},{8,10},{10,8},{12,14},{14,12},{1,3},{3,1},... | collective-permute-start | bytes 786440 | tf_op jit(solution)/shard_map/ppermute | solution.py:24
  366.4 14.7 %collective-permute-start.2 = (bf16[1,8,8,2048]{3,2,1,0:T(8,128)(2,1)S(1)}, bf16[1,8,8,2048]{3,2,1,0:T(8,128)(2,1)S(1)}, u32[]{:S(2)}, u32[]{:S(2)}) collective-permute-start(bf16[1,8,8,2048]{3,2,1,0:T(8,128)(2,1)S(1)} %copy.103), channel_id=1, source_target_pairs={{0,4},{2,6},{4,0},{6,2},{8,12},{10,14},{12,8},{14,10},{1,5},{3,7},... | collective-permute-start | bytes 786440 | tf_op jit(solution)/shard_map/ppermute | solution.py:24
  368.5 17.3 %collective-permute-start.3 = (bf16[1,8,8,2048]{3,2,1,0:T(8,128)(2,1)S(1)}, bf16[1,8,8,2048]{3,2,1,0:T(8,128)(2,1)S(1)}, u32[]{:S(2)}, u32[]{:S(2)}) collective-permute-start(bf16[1,8,8,2048]{3,2,1,0:T(8,128)(2,1)S(1)} %copy.104), channel_id=1, source_target_pairs={{0,6},{2,4},{4,2},{6,0},{8,14},{10,12},{12,10},{14,8},{1,7},{3,5},... | collective-permute-start | bytes 786440 | tf_op jit(solution)/shard_map/ppermute | solution.py:24
  370.2 29.7 %collective-permute-start.4 = (bf16[1,8,8,2048]{3,2,1,0:T(8,128)(2,1)S(1)}, bf16[1,8,8,2048]{3,2,1,0:T(8,128)(2,1)S(1)}, u32[]{:S(2)}, u32[]{:S(2)}) collective-permute-start(bf16[1,8,8,2048]{3,2,1,0:T(8,128)(2,1)S(1)} %copy.105), channel_id=1, source_target_pairs={{0,8},{2,10},{4,12},{6,14},{8,0},{10,2},{12,4},{14,6},{1,9},{3,11}... | collective-permute-start | bytes 786440 | tf_op jit(solution)/shard_map/ppermute | solution.py:24
  373.4 32.4 %collective-permute-start.5 = (bf16[1,8,8,2048]{3,2,1,0:T(8,128)(2,1)S(1)}, bf16[1,8,8,2048]{3,2,1,0:T(8,128)(2,1)S(1)}, u32[]{:S(2)}, u32[]{:S(2)}) collective-permute-start(bf16[1,8,8,2048]{3,2,1,0:T(8,128)(2,1)S(1)} %copy.106), channel_id=1, source_target_pairs={{0,10},{2,8},{4,14},{6,12},{8,2},{10,0},{12,6},{14,4},{1,11},{3,9}... | collective-permute-start | bytes 786440 | tf_op jit(solution)/shard_map/ppermute | solution.py:24
  374.3 31.6 %collective-permute-start.6 = (bf16[1,8,8,2048]{3,2,1,0:T(8,128)(2,1)S(1)}, bf16[1,8,8,2048]{3,2,1,0:T(8,128)(2,1)S(1)}, u32[]{:S(2)}, u32[]{:S(2)}) collective-permute-start(bf16[1,8,8,2048]{3,2,1,0:T(8,128)(2,1)S(1)} %copy.107), channel_id=1, source_target_pairs={{0,12},{2,14},{4,8},{6,10},{8,4},{10,6},{12,0},{14,2},{1,13},{3,15... | collective-permute-start | bytes 786440 | tf_op jit(solution)/shard_map/ppermute | solution.py:24
  381.1 24.8 %collective-permute-start.7 = (bf16[1,8,8,2048]{3,2,1,0:T(8,128)(2,1)S(1)}, bf16[1,8,8,2048]{3,2,1,0:T(8,128)(2,1)S(1)}, u32[]{:S(2)}, u32[]{:S(2)}) collective-permute-start(bf16[1,8,8,2048]{3,2,1,0:T(8,128)(2,1)S(1)} %copy.108), channel_id=1, source_target_pairs={{0,14},{2,12},{4,10},{6,8},{8,6},{10,4},{12,2},{14,0},{1,15},{3,13... | collective-permute-start | bytes 786440 | tf_op jit(solution)/shard_map/ppermute | solution.py:24
  415.1 12.5 %copy-start.14 = (s32[16]{0:T(128)S(1)}, s32[16]{0:T(128)}, u32[]{:S(2)}) copy-start(s32[16]{0:T(128)} %param.32) | copy-start | bytes 196
  416.7 17.3 %all-to-all-start = ((bf16[8,8,16]{2,1,0:T(8,128)(2,1)}), bf16[8,8,16]{2,1,0:T(8,128)(2,1)S(1)}, u32[]{:S(2)}, u32[]{:S(2)}) async-start(bf16[8,8,16]{2,1,0:T(8,128)(2,1)} %bitcast.19), calls=%async_computation | async-start | bytes 32768 | tf_op jit(solution)/shard_map/all_to_all | solution.py:214
  427.7 16.2 %copy-start.16 = (f32[2048]{0:T(1024)S(1)}, f32[2048]{0:T(1024)}, u32[]{:S(2)}) copy-start(f32[2048]{0:T(1024)} %param.28) | copy-start | bytes 24580
  453.5 54.5 %all-to-all-start.1 = ((bf16[8,8,8,2048]{3,2,1,0:T(8,128)(2,1)}), bf16[8,8,8,2048]{3,2,1,0:T(8,128)(2,1)S(1)}, u32[]{:S(2)}, u32[]{:S(2)}) async-start(bf16[8,8,8,2048]{3,2,1,0:T(8,128)(2,1)} %bitcast.176), calls=%async_computation.1 | async-start | bytes 4194304 | tf_op jit(solution)/shard_map/all_to_all | solution.py:232
  (16 other events, 32.8 us)
Sparse Core Ops, SparseCore 0:
  415.3 27.4 all-reduce.3
